TPU v7x, 32 devices: a whole 2x2x4 slice. The times are simulated.
32 devices in a mesh: segment: 8 (over z, core), head: 4 (over y, x).
Axes of the slice: x: 2, y: 2, z: 4, core: 2. Of those that a mesh axis runs over, the one named last changes fastest.
Arguments:
- slices: bfloat16 [1024, 4096], P('segment', 'head'), may hold values from -6 to 6
- new_slice: bfloat16 [128, 4096], P(None, 'head'), may hold values from -6 to 6
- norm_gain: float32 [8, 4096], P('segment'), may hold values from 0.1 to 1.9
- w_query: bfloat16 [8, 4096, 2048], P('segment', None, 'head'), may hold values from -0.09375 to 0.09375
- w_keyval: bfloat16 [8, 4096, 1024], P('segment', None, 'head'), may hold values from -0.1875 to 0.1875
- w_out: bfloat16 [8, 2048, 4096], P('segment', 'head'), may hold values from -0.375 to 0.375
- cached_rows: bfloat16 [8, 16384, 256], P('segment', 'head'), may hold values from -400 to 400
- lengths: int32 [8], P('segment'), may hold values from 256 to 4096
Outputs:
- first_pass: float32 [1024, 4096], P('segment', 'head')
- second_pass: float32 [1024, 4096], P('segment', 'head')
All inputs are finite; a program needn't handle non-finite values.
Results may differ from a plain program's by a relative error of at most 0.029.
The roundings to bfloat16 on the way count: a program that leaves them out, or rounds other values in their place, can miss the bound.
Values may be sent and summed in bfloat16 or wider, within the bound.
A program may use at most 64 MiB of HBM per device.

v0:
```python
import jax
import jax.numpy as jnp
from jax import lax
from jax.sharding import PartitionSpec as P

KVH = 4
HD = 128


EPSILON = 1e-05
ROPE_BASE = 1000000.0
NEGATIVE = -1e30


def swapped(block, axis, bit):
    count = lax.axis_size(axis)
    route = []
    for low in range(count):
        high = low | 1 << bit
        if high != low and high < count:
            route += [(low, high), (high, low)]
    return lax.ppermute(block, axis, route)


def from_behind(shard, axis, by):
    peers = lax.axis_size(axis)
    pairs = [(i, i + by) for i in range(peers) if 0 <= i + by < peers]
    return lax.ppermute(shard, axis, pairs)


def rotate(entries, positions):
    half_dim = entries.shape[-1] // 2
    exponent = jnp.arange(half_dim, dtype=jnp.float32) * (2.0 / entries.shape[-1])
    inverse = jnp.power(jnp.float32(ROPE_BASE), -exponent)
    angles = positions[:, None] * inverse[None, :]
    cosine = jnp.cos(angles)[:, None, :]
    sine = jnp.sin(angles)[:, None, :]
    first_half = entries[..., :half_dim]
    second_half = entries[..., half_dim:]
    return jnp.concatenate(
        [first_half * cosine - second_half * sine, second_half * cosine + first_half * sine],
        axis=-1,
    )


def normalize(rows_in, gain_vector):
    mean_square = jnp.mean(rows_in * rows_in, axis=-1, keepdims=True)
    return (rows_in * lax.rsqrt(mean_square + EPSILON) * gain_vector).astype(jnp.bfloat16)


def combine_partial(left_side, right_side):
    left_peak, left_total, left_out = left_side
    right_peak, right_total, right_out = right_side
    joined = jnp.maximum(left_peak, right_peak)
    left_scale = jnp.exp(left_peak - joined)
    right_scale = jnp.exp(right_peak - joined)
    return (
        joined,
        left_scale * left_total + right_scale * right_total,
        left_scale[..., None] * left_out + right_scale[..., None] * right_out,
    )


def softmax_partial(queries, key_rows, value_rows, visible):
    scores = jnp.einsum(
        "rnd,kd->nrk", queries, key_rows, preferred_element_type=jnp.float32
    ) * HD ** (-0.5)
    scores = jnp.where(visible[None], scores, NEGATIVE)
    row_peak = jnp.max(scores, axis=-1)
    weights = jnp.where(visible[None], jnp.exp(scores - row_peak[..., None]), 0.0)
    row_total = jnp.sum(weights, axis=-1)
    outputs = jnp.einsum(
        "nrk,kd->nrd", weights.astype(jnp.bfloat16), value_rows, preferred_element_type=jnp.float32
    )
    return (row_peak, row_total, outputs)


def blank_partial(head_total, row_total):
    return (
        jnp.full((head_total, row_total), NEGATIVE, jnp.float32),
        jnp.zeros((head_total, row_total), jnp.float32),
        jnp.zeros((head_total, row_total, HD), jnp.float32),
    )


def attend_range(query_set, key_table, low_bound, high_bound, block_rows):
    row_total = query_set.shape[0]
    first_block = low_bound // block_rows
    last_block = (high_bound + block_rows - 1) // block_rows

    def one_block(turn_index, running):
        block_start = (first_block + turn_index) * block_rows
        key_piece = lax.dynamic_slice_in_dim(key_table, block_start, block_rows, 0)
        places = block_start + jnp.arange(block_rows, dtype=jnp.int32)
        live_mask = (places >= low_bound) & (places < high_bound)
        visible = jnp.broadcast_to(live_mask[None, :], (row_total, block_rows))
        return combine_partial(
            running, softmax_partial(query_set, key_piece[:, :HD], key_piece[:, HD:], visible)
        )

    turns = jnp.maximum(last_block - first_block, 0)
    return lax.fori_loop(0, turns, one_block, blank_partial(query_set.shape[1], row_total))


def local(slices, new_slice, norm_gain, w_query, w_keyval, w_out, cached_rows, lengths):
    segment_index = lax.axis_index("segment")
    head_index = lax.axis_index("head")
    head_count = lax.axis_size("head")
    row_count, width = slices.shape
    group_size = head_count // KVH
    bit_count = group_size.bit_length() - 1
    position = head_index % group_size
    local_heads = w_query.shape[2] // HD
    length = lengths[0]
    gain_vector = norm_gain[0]
    query_w = w_query[0]
    keyval_w = w_keyval[0]
    out_w = w_out[0]
    cache_rows = cached_rows[0]
    row_ids = jnp.arange(row_count, dtype=jnp.int32)
    causal = row_ids[:, None] >= row_ids[None, :]
    assembled = cache_rows
    for bit_number in range(bit_count):
        partner_rows = swapped(assembled, "head", bit_number)
        high_bit = position // (1 << bit_number) % 2
        assembled = jnp.where(
            high_bit == 0,
            jnp.concatenate([assembled, partner_rows], axis=0),
            jnp.concatenate([partner_rows, assembled], axis=0),
        )
    table_rows = assembled.shape[0]
    block_rows = min(512, table_rows // 4)
    own_live = jnp.clip(length, 0, table_rows)

    def cache_partial(query_set):
        combined = attend_range(query_set, assembled, 0, own_live, block_rows)
        return combined

    def project(full_rows, offset):
        normed = normalize(full_rows, gain_vector)
        positions = (length + offset + row_ids).astype(jnp.float32)
        queries = jnp.dot(normed, query_w, preferred_element_type=jnp.float32).reshape(
            row_count, local_heads, HD
        )
        queries = rotate(queries, positions).astype(jnp.bfloat16)
        chosen = jnp.dot(normed, keyval_w, preferred_element_type=jnp.float32)
        for bit_number in range(bit_count):
            partner_part = swapped(chosen, "head", bit_number)
            high_bit = position // (1 << bit_number) % 2
            chosen = jnp.where(
                high_bit == 0,
                jnp.concatenate([chosen, partner_part], axis=1),
                jnp.concatenate([partner_part, chosen], axis=1),
            )
        new_keys = rotate(chosen[:, None, :HD], positions)[:, 0].astype(jnp.bfloat16)
        new_values = chosen[:, HD:].astype(jnp.bfloat16)
        return (queries, new_keys, new_values)

    def attend(queries, new_keys, new_values, earlier):
        if earlier is None:
            recent_keys = new_keys
            recent_values = new_values
            recent_live = causal
        else:
            recent_keys = jnp.concatenate([earlier[0], new_keys], axis=0)
            recent_values = jnp.concatenate([earlier[1], new_values], axis=0)
            recent_live = jnp.concatenate([jnp.ones((row_count, row_count), bool), causal], axis=1)
        running = cache_partial(queries)
        recent = softmax_partial(queries, recent_keys, recent_values, recent_live)
        row_peak, row_total, outputs = combine_partial(running, recent)
        attended = (outputs / row_total[..., None]).astype(jnp.bfloat16).transpose(1, 0, 2)
        return attended.reshape(row_count, local_heads * HD)

    def mix(full_rows, offset, earlier):
        queries, new_keys, new_values = project(full_rows, offset)
        attended = attend(queries, new_keys, new_values, earlier)
        return (
            jnp.dot(attended, out_w, preferred_element_type=jnp.float32),
            (new_keys, new_values),
        )

    def advance(own_rows, offset, earlier):
        full_rows = lax.all_gather(own_rows, "head", axis=1, tiled=True)
        partial_out, recent = mix(full_rows, offset, earlier)
        summed = lax.psum_scatter(partial_out, "head", scatter_dimension=1, tiled=True)
        return (own_rows + summed, recent)

    first_out, recent = advance(slices.astype(jnp.float32), 0, None)
    arrived = from_behind(first_out, "segment", 1)
    entering = jnp.where(segment_index == 0, new_slice.astype(jnp.float32), arrived)
    second_out, _ = advance(entering, row_count, recent)
    return (first_out, second_out)


def solution(mesh):
    placed = (
        P("segment", "head"),
        P(None, "head"),
        P("segment", None),
        P("segment", None, "head"),
        P("segment", None, "head"),
        P("segment", "head", None),
        P("segment", "head", None),
        P("segment"),
    )
    return jax.shard_map(
        local,
        mesh=mesh,
        in_specs=placed,
        out_specs=(P("segment", "head"), P("segment", "head")),
        check_vma=False,
    )
```

profile of v0, /device:TPU:0, one launch (start us, length us, event | category | flops | bytes accessed | tf_op | source)
XLA Modules:
  0.0 281.0 jit_solution(5658598250094640011)
XLA Ops:
  7.2 1.9 convert_element_type.56
  9.9 6.4 %copy.60 = bf16[512,4096]{1,0:T(8,128)(2,1)} copy(bf16[512,4096]{0,1:T(8,128)(2,1)} %bitcast.103) | data formatting | bytes 8388608 | tf_op jit(solution)/shard_map/dot_general | solution.py:142
  17.9 30.6 %all-gather.3.cloned.1.call-done = f32[128,4096]{1,0:T(8,128)} async-done(((f32[128,1024]{1,0:T(8,128)}), f32[128,4096]{1,0:T(8,128)}) %all-gather.3.cloned.1.call-update) | async-done | bytes 2097168 | tf_op jit(solution)/shard_map/all_gather | solution.py:183
  48.5 2.0 multiply_reduce_fusion.1
  52.8 4.1 %fusion.48 = f32[128,4,128]{0,2,1:T(8,128)S(1)} fusion(bf16[4,128,4096]{2,1,0:T(8,128)(2,1)} %bitcast.101, f32[128,4096]{1,0:T(8,128)} %all-gather.3.cloned.1.call-done, f32[4096]{0:T(1024)S(1)} %bitcast.106, f32[128]{0:T(128)S(1)} %add_rsqrt_fusion.1), kind=kOutput, calls=%fused_computation.72 | convolution fusion | flops 538443776 | bytes 6570496 | tf_op jit(solution)/shard_map/dot_general | solution.py:142
  59.0 21.0 %while.28 = (s32[]{:T(128)}, f32[4,128]{1,0:T(4,128)}, f32[4,128]{1,0:T(4,128)}, f32[4,128,128]{2,1,0:T(8,128)S(1)}, s32[]{:T(128)}, /*index=5*/s32[]{:T(128)}, ...) while((s32[]{:T(128)}, f32[4,128]{1,0:T(4,128)}, ...), condition=%wide.region_4.5_spmd, body=%wide.region_1.4_spmd.sunk | while | flops 136777728 | bytes 4127035 | solution.py:102
  59.1 1.2 fusion.124
  61.7 1.5 fusion.126
  63.3 1.2 fusion.124
  65.9 1.5 fusion.126
  67.5 1.2 fusion.124
  70.1 1.5 fusion.126
  74.3 1.5 fusion.126
  78.5 1.5 fusion.126
  83.9 4.3 %fusion.30 = f32[128,4096]{1,0:T(8,128)} fusion(bf16[128,512]{0,1:T(8,128)(2,1)S(1)} %bitcast.112, bf16[1,512,4096]{2,1,0:T(8,128)(2,1)} %param.17), kind=kOutput, calls=%fused_computation.46 | convolution fusion | flops 536870912 | bytes 6422528 | tf_op jit(solution)/shard_map/dot_general | solution.py:178
  88.2 47.9 %reduce-scatter.3.cloned.1.call-done = f32[128,1024]{1,0:T(8,128)} async-done(((f32[128,4096]{1,0:T(8,128)}), f32[128,1024]{1,0:T(8,128)}) %reduce-scatter.3.cloned.1.call-update) | async-done | bytes 524304 | tf_op jit(solution)/shard_map/reduce_scatter | solution.py:185
  137.2 1.9 collective-permute-start
  139.2 1.5 collective-permute-done
  142.2 1.4 slice.93
  144.3 40.0 %all-gather.5.cloned.1.call-done = f32[128,4096]{1,0:T(8,128)} async-done(((f32[128,1024]{1,0:T(8,128)}), f32[128,4096]{1,0:T(8,128)}) %all-gather.5.cloned.1.call-update) | async-done | bytes 2097168 | tf_op jit(solution)/shard_map/all_gather | solution.py:183
  184.2 2.0 multiply_reduce_fusion
  188.6 4.1 %fusion.46 = f32[128,4,128]{0,2,1:T(8,128)S(1)} fusion(bf16[4,128,4096]{2,1,0:T(8,128)(2,1)} %bitcast.102, f32[128,4096]{1,0:T(8,128)} %all-gather.5.cloned.1.call-done, f32[128]{0:T(128)S(1)} %add_rsqrt_fusion, f32[4096]{0:T(1024)S(1)} %bitcast.108), kind=kOutput, calls=%fused_computation.70 | convolution fusion | flops 538443776 | bytes 6570496 | tf_op jit(solution)/shard_map/dot_general | solution.py:142
  194.8 20.9 %while.29 = (s32[]{:T(128)}, f32[4,128]{1,0:T(4,128)}, f32[4,128]{1,0:T(4,128)}, f32[4,128,128]{2,1,0:T(8,128)S(1)}, s32[]{:T(128)}, /*index=5*/s32[]{:T(128)}, ...) while((s32[]{:T(128)}, f32[4,128]{1,0:T(4,128)}, ...), condition=%wide.region_12.13_spmd, body=%wide.region_9.12_spmd.sunk | while | flops 136777728 | bytes 4127035 | solution.py:102
  197.4 1.5 fusion.132
  199.0 1.2 fusion.130
  201.6 1.5 fusion.132
  205.8 1.5 fusion.132
  210.0 1.5 fusion.132
  214.2 1.5 fusion.132
  220.3 4.3 %fusion.28 = f32[128,4096]{1,0:T(8,128)} fusion(bf16[128,512]{0,1:T(8,128)(2,1)S(1)} %bitcast.111, bf16[1,512,4096]{2,1,0:T(8,128)(2,1)} %param.17), kind=kOutput, calls=%fused_computation.44 | convolution fusion | flops 536870912 | bytes 6422528 | tf_op jit(solution)/shard_map/dot_general | solution.py:178
  224.6 47.9 %reduce-scatter.5.cloned.1.call-done = f32[128,1024]{1,0:T(8,128)} async-done(((f32[128,4096]{1,0:T(8,128)}), f32[128,1024]{1,0:T(8,128)}) %reduce-scatter.5.cloned.1.call-update) | async-done | bytes 524304 | tf_op jit(solution)/shard_map/reduce_scatter | solution.py:185
  272.6 1.9 add.131
  (212 shorter events, 43.5 us)
Async XLA Ops:
  7.2 43.3 %copy-start = (bf16[1,4096,256]{2,1,0:T(8,128)(2,1)S(1)}, bf16[1,4096,256]{2,1,0:T(8,128)(2,1)}, u32[]{:S(2)}) copy-start(bf16[1,4096,256]{2,1,0:T(8,128)(2,1)} %param.16) | copy-start | bytes 6291460
  7.2 41.3 %all-gather.3.cloned.1.call-start = ((), (), s32[]{:S(2)}) async-start(), calls=%async_computation.2 | async-start | bytes 2621440 | tf_op jit(solution)/shard_map/all_gather | solution.py:183
  9.2 126.9 %reduce-scatter.3.cloned.1.call-start = ((), (), s32[]{:S(2)}) async-start(), calls=%async_computation.3 | async-start | bytes 2621440 | tf_op jit(solution)/shard_map/reduce_scatter | solution.py:185
  16.3 34.1 %copy-start.7 = (f32[1,4096]{1,0:T(1,128)S(1)}, f32[1,4096]{1,0:T(1,128)}, u32[]{:S(2)}) copy-start(f32[1,4096]{1,0:T(1,128)} %param.14) | copy-start | bytes 49156
  16.3 35.7 %copy-start.27 = (f32[64]{0:T(128)}, f32[64]{0:T(128)S(1)}, u32[]{:S(2)}) copy-start(f32[64]{0:T(128)S(1)} %negate_power_fusion) | copy-start | bytes 772
  16.4 34.9 %copy-start.29 = (f32[128]{0:T(128)}, f32[128]{0:T(128)S(1)}, u32[]{:S(2)}) copy-start(f32[128]{0:T(128)S(1)} %get-tuple-element.198) | copy-start | bytes 1540
  48.5 2.2 copy-start.1
  63.2 1.5 copy-start.21
  63.2 1.5 copy-start.23
  67.4 1.5 copy-start.21
  67.4 1.5 copy-start.23
  71.6 1.5 copy-start.21
  75.8 1.5 copy-start.21
  75.8 1.5 copy-start.23
  88.1 48.0 %copy-start.4 = (bf16[128,1024]{1,0:T(8,128)(2,1)S(1)}, bf16[128,1024]{1,0:T(8,128)(2,1)}, u32[]{:S(2)}) copy-start(bf16[128,1024]{1,0:T(8,128)(2,1)} %param.12) | copy-start | bytes 786436
  88.1 52.5 %copy-start.9 = (bf16[128,1024]{1,0:T(8,128)(2,1)S(1)}, bf16[128,1024]{1,0:T(8,128)(2,1)}, u32[]{:S(2)}) copy-start(bf16[128,1024]{1,0:T(8,128)(2,1)} %param.13) | copy-start | bytes 786436
  88.2 53.4 %copy-start.14 = (pred[128,128]{0,1:T(8,128)(4,1)S(1)}, pred[128,128]{0,1:T(8,128)(4,1)}, u32[]{:S(2)}) copy-start(pred[128,128]{0,1:T(8,128)(4,1)} %iota_compare_fusion) | copy-start | bytes 49156
  88.2 55.5 %copy-start.25 = (bf16[128,1,64]{0,2,1:T(8,128)(2,1)S(1)}, bf16[128,1,64]{0,2,1:T(8,128)(2,1)}, u32[]{:S(2)}) copy-start(bf16[128,1,64]{0,2,1:T(8,128)(2,1)} %get-tuple-element.186) | copy-start | bytes 49156
  88.2 55.5 %copy-start.26 = (bf16[128,1,64]{0,2,1:T(8,128)(2,1)S(1)}, bf16[128,1,64]{0,2,1:T(8,128)(2,1)}, u32[]{:S(2)}) copy-start(bf16[128,1,64]{0,2,1:T(8,128)(2,1)} %get-tuple-element.187) | copy-start | bytes 49156
  88.2 96.0 %all-gather.5.cloned.1.call-start = ((), (), s32[]{:S(2)}) async-start(), calls=%async_computation.4 | async-start | bytes 2621440 | tf_op jit(solution)/shard_map/all_gather | solution.py:183
  137.2 49.8 %copy-start.5 = (f32[128,1024]{1,0:T(8,128)}, f32[128,1024]{1,0:T(8,128)S(1)}, u32[]{:S(2)}) copy-start(f32[128,1024]{1,0:T(8,128)S(1)} %convert_add_fusion) | copy-start | bytes 1572868
  137.2 49.0 %copy-start.8 = (f32[1,4096]{1,0:T(1,128)S(1)}, f32[1,4096]{1,0:T(1,128)}, u32[]{:S(2)}) copy-start(f32[1,4096]{1,0:T(1,128)} %param.14) | copy-start | bytes 49156
  137.2 3.4 %collective-permute-start = (f32[128,1024]{1,0:T(8,128)S(1)}, f32[128,1024]{1,0:T(8,128)S(1)}, u32[]{:S(2)}, u32[]{:S(2)}) collective-permute-start(f32[128,1024]{1,0:T(8,128)S(1)} %convert_add_fusion), channel_id=1, source_target_pairs={{0,4},{4,8},{8,12},{12,16},{16,20},{20,24},{24,28},{1,5},{5,9},{9,... | collective-permute-start | bytes 1572872 | tf_op jit(solution)/shard_map/ppermute | solution.py:28
  141.5 131.0 %reduce-scatter.5.cloned.1.call-start = ((), (), s32[]{:S(2)}) async-start(), calls=%async_computation.5 | async-start | bytes 2621440 | tf_op jit(solution)/shard_map/reduce_scatter | solution.py:185
  184.2 2.2 copy-start.2
  188.6 4.2 %copy-start.15 = (f32[128,64]{0,1:T(8,128)S(1)}, f32[128,64]{0,1:T(8,128)}, u32[]{:S(2)}) copy-start(f32[128,64]{0,1:T(8,128)} %get-tuple-element.188) | copy-start | bytes 98308
  188.6 4.2 %copy-start.16 = (f32[128,64]{0,1:T(8,128)S(1)}, f32[128,64]{0,1:T(8,128)}, u32[]{:S(2)}) copy-start(f32[128,64]{0,1:T(8,128)} %get-tuple-element.189) | copy-start | bytes 98308
  198.9 1.5 copy-start.17
  198.9 1.5 copy-start.19
  207.3 1.5 copy-start.17
  207.3 1.5 copy-start.19
  224.6 48.0 %copy-start.3 = (f32[128,1024]{1,0:T(8,128)S(1)}, f32[128,1024]{1,0:T(8,128)}, u32[]{:S(2)}) copy-start(f32[128,1024]{1,0:T(8,128)} %convert_select_fusion) | copy-start | bytes 1572868
  (36 other events, 30.6 us)
Sparse Core Ops, SparseCore 0:
  10.4 38.0 all-gather.2
  88.3 47.7 reduce-scatter.2
  141.6 42.5 all-gather.4
  224.8 47.7 reduce-scatter.4
where the time goes:
time: 281 us
  waiting for transfers between devices  168 us (60%)
  matrix products  49.4 us (18%)
  local copies, waits for them, and re-layouts  26.3 us (9%)
  other arithmetic  19.8 us (7%)
  between operations  14.8 us (5%)
    reduce_scatter x2, waiting for transfers between devices, advance(): lax.psum_scatter(partial_out, 'head', scatter_dimension=1, tiled=True)  95.8 us
    all_gather x2, waiting for transfers between devices, advance(): full_rows = lax.all_gather(own_rows, 'head', axis=1, tiled=True)  70.5 us
    dot_general x12, matrix products, softmax_partial(): jnp.einsum('nrk,kd->nrd', weights.astype(jnp.bfloat16), value_rows, prefe...  16.9 us
    dot_general x12, matrix products, softmax_partial(): jnp.einsum('rnd,kd->nrk', queries, key_rows, preferred_element_type=jnp.f...  14.6 us
    while x80, local copies, waits for them, and re-layouts  11.7 us
    dot_general x2, matrix products, mix(): jnp.dot(attended, out_w, preferred_element_type=jnp.float32)  8.55 us
    dot_general x2, matrix products, project(): jnp.dot(normed, query_w, preferred_element_type=jnp.float32)  8.28 us
    dot_general x1, local copies, waits for them, and re-layouts, project(): jnp.dot(normed, query_w, preferred_element_type=jnp.float32)  6.43 us
  transfers between devices with their start and end apart: 5, of which 5 were waited for; matrix products, arithmetic and copies ran while one was open for 4% of the time, Pallas kernels for 0%

commit v1 on v0

--- a/solution.py
+++ b/solution.py
@@ -1,10 +1,15 @@
+import functools
+
 import jax
 import jax.numpy as jnp
 from jax import lax
+from jax.experimental import pallas as pl
+from jax.experimental.pallas import tpu as pltpu
 from jax.sharding import PartitionSpec as P
 
 KVH = 4
 HD = 128
+MESH = pl.DeviceIdType.MESH
 
 
 EPSILON = 1e-05
@@ -192,6 +197,366 @@
     return (first_out, second_out)
 
 
+def exchange_kernel(
+    row_chunks, x_ref, new_ref, gain_ref, cos_ref, sin_ref, len_ref, wq_hbm, wkv_hbm, wo_hbm, cache_hbm,
+    first_ref, second_ref,
+    wq, wkv, wo, cache, gathered, normed, q_buf, score_buf, mask_buf, new_k, new_v, att_buf,
+    diag_send, x_send, y_send, keep_x, keep_y, keep_own, diag_x_land, diag_y_land, x_land, y_land,
+    forward_buf, load_sem, send_sem, recv_sem,
+):
+    seg = lax.axis_index("segment")
+    me = lax.axis_index("head")
+    seg_count = lax.axis_size("segment")
+    x_peer = me + 1 - 2 * (me % 2)
+    y_peer = (me + 2) % 4
+    far_peer = x_peer + 2 - 4 * (x_peer // 2)
+    rows, features = x_ref.shape
+    blocks = gathered.shape[1]
+    chunk = rows // row_chunks
+    half = chunk // 2
+    local_heads = wq.shape[1] // HD
+    cached = cache.shape[0]
+    key_block = min(512, cached)
+    exponent_scale = HD ** (-0.5) * 1.4426950408889634
+
+    loads = [
+        pltpu.make_async_copy(source, target, load_sem.at[i])
+        for i, (source, target) in enumerate(
+            [(wq_hbm.at[0], wq), (wkv_hbm.at[0], wkv), (cache_hbm.at[0], cache), (wo_hbm.at[0], wo)]
+        )
+    ]
+    for load in loads:
+        load.start()
+
+    gathered[0, me] = x_ref[...]
+
+    barrier = pltpu.get_barrier_semaphore()
+    for peer in (x_peer, y_peer):
+        pl.semaphore_signal(barrier, inc=1, device_id={"head": peer}, device_id_type=MESH)
+
+    @pl.when(seg > 0)
+    def _():
+        pl.semaphore_signal(barrier, inc=1, device_id={"segment": seg - 1}, device_id_type=MESH)
+
+    @pl.when(seg < seg_count - 1)
+    def _():
+        pl.semaphore_signal(barrier, inc=1, device_id={"segment": seg + 1}, device_id_type=MESH)
+
+    before = (seg + seg_count - 1) // seg_count
+    after = (2 * seg_count - 2 - seg) // seg_count
+    pl.semaphore_wait(barrier, 2 + before + after)
+
+    copies = []
+
+    def remote(source, target, where):
+        at = len(copies)
+        made = pltpu.make_async_remote_copy(
+            src_ref=source, dst_ref=target, send_sem=send_sem.at[at], recv_sem=recv_sem.at[at],
+            device_id=where, device_id_type=MESH,
+        )
+        copies.append(made)
+        return made
+
+    def low(c):
+        return pl.ds(c * chunk, half)
+
+    def high(c):
+        return pl.ds(c * chunk + half, half)
+
+    gather_copies = {}
+
+    def gather_send(p, c):
+        made = []
+        for part in (low(c), high(c)):
+            own = gathered.at[p, me, part]
+            made.append(remote(own, own, {"head": x_peer}))
+        for part in (high(c), low(c)):
+            own = gathered.at[p, me, part]
+            made.append(remote(own, own, {"head": y_peer}))
+        gather_copies[p, c] = made
+        for at in (0, 2, 1, 3):
+            made[at].start()
+
+    def gather_pass_on(p, c):
+        made = gather_copies[p, c]
+        made[0].wait_recv()
+        from_x = gathered.at[p, x_peer, low(c)]
+        made.append(remote(from_x, from_x, {"head": y_peer}))
+        made[4].start()
+        made[2].wait_recv()
+        from_y = gathered.at[p, y_peer, high(c)]
+        made.append(remote(from_y, from_y, {"head": x_peer}))
+        made[5].start()
+
+    def rope(entries, table_rows):
+        return entries * cos_ref[table_rows] + pltpu.roll(entries, HD // 2, 1) * sin_ref[table_rows]
+
+    def project(p, c):
+        made = gather_copies[p, c]
+        for at in (1, 3, 4, 5):
+            made[at].wait_recv()
+        part = pl.ds(c * chunk, chunk)
+        total = jnp.zeros((chunk, 1), jnp.float32)
+        for b in range(blocks):
+            piece = gathered[p, b, part].astype(jnp.float32)
+            total = total + jnp.sum(piece * piece, axis=-1, keepdims=True)
+        scale = lax.rsqrt(total / (blocks * features) + EPSILON)
+        for b in range(blocks):
+            piece = gathered[p, b, part].astype(jnp.float32)
+            columns = pl.ds(b * features, features)
+            normed[:, columns] = (piece * scale * gain_ref[:, columns]).astype(jnp.bfloat16)
+        table_rows = pl.ds(p * rows + c * chunk, chunk)
+        if p == 0 and c == 0:
+            loads[0].wait()
+            loads[1].wait()
+        queries = jnp.dot(normed[...], wq[...], preferred_element_type=jnp.float32)
+        for j in range(local_heads):
+            turned = rope(queries[:, j * HD:(j + 1) * HD], table_rows)
+            q_buf[pl.ds(j * chunk, chunk)] = turned.astype(jnp.bfloat16)
+        chosen = jnp.dot(normed[...], wkv[...], preferred_element_type=jnp.float32)
+        new_k[p, part] = rope(chosen[:, :HD], table_rows).astype(jnp.bfloat16)
+        new_v[p, part] = chosen[:, HD:].astype(jnp.bfloat16)
+
+    def attend(p, c):
+        if p == 0 and c == 0:
+            loads[2].wait()
+        queries = q_buf[...]
+        count = local_heads * chunk
+
+        def product(keys):
+            return lax.dot_general(
+                queries, keys, (((1,), (1,)), ((), ())), preferred_element_type=jnp.float32
+            )
+
+        peak = jnp.full((count, HD), NEGATIVE, jnp.float32)
+        for start in range(0, cached, key_block):
+            scores = product(cache[pl.ds(start, key_block), pl.ds(0, HD)])
+            scores = scores + mask_buf[:, pl.ds(start, key_block)]
+            score_buf[:, pl.ds(start, key_block)] = scores
+            for lane in range(0, key_block, HD):
+                peak = jnp.maximum(peak, scores[:, lane:lane + HD])
+        recents = []
+        for earlier in range(p):
+            recents.append((product(new_k[earlier]), earlier))
+        scores = product(new_k[p])
+        row_at = lax.broadcasted_iota(jnp.int32, scores.shape, 0) % chunk + c * chunk
+        key_at = lax.broadcasted_iota(jnp.int32, scores.shape, 1)
+        recents.append((jnp.where(key_at <= row_at, scores, NEGATIVE), p))
+        for scores, _ in recents:
+            peak = jnp.maximum(peak, scores)
+        top = jnp.max(peak, axis=-1, keepdims=True)
+        sums = jnp.zeros((count, HD), jnp.float32)
+        outputs = jnp.zeros((count, HD), jnp.float32)
+        for scores, which in recents:
+            weights = jnp.exp2((scores - top) * exponent_scale)
+            sums = sums + weights
+            outputs = outputs + jnp.dot(
+                weights.astype(jnp.bfloat16), new_v[which], preferred_element_type=jnp.float32
+            )
+        for start in range(0, cached, key_block):
+            weights = jnp.exp2((score_buf[:, pl.ds(start, key_block)] - top) * exponent_scale)
+            for lane in range(0, key_block, HD):
+                sums = sums + weights[:, lane:lane + HD]
+            outputs = outputs + jnp.dot(
+                weights.astype(jnp.bfloat16), cache[pl.ds(start, key_block), pl.ds(HD, HD)],
+                preferred_element_type=jnp.float32,
+            )
+        attended = (outputs / jnp.sum(sums, axis=-1, keepdims=True)).astype(jnp.bfloat16)
+        for j in range(local_heads):
+            att_buf[:, pl.ds(j * HD, HD)] = attended[j * chunk:(j + 1) * chunk]
+
+    scatter_copies = {}
+
+    def mix(p, c):
+        if p == 0 and c == 0:
+            loads[3].wait()
+        part = pl.ds(c * chunk, chunk)
+
+        def partial(owner):
+            columns = pl.ds(pl.multiple_of(owner * features, features), features)
+            return jnp.dot(att_buf[...], wo[:, columns], preferred_element_type=jnp.float32)
+
+        diag_send[p, part] = partial(far_peer).astype(jnp.bfloat16)
+        made = [
+            remote(diag_send.at[p, low(c)], diag_x_land.at[p, c], {"head": x_peer}),
+            remote(diag_send.at[p, high(c)], diag_y_land.at[p, c], {"head": y_peer}),
+        ]
+        made[0].start()
+        made[1].start()
+        for_x = partial(x_peer)
+        x_send[p, low(c)] = for_x[:half].astype(jnp.bfloat16)
+        keep_x[c] = for_x[half:]
+        made.append(remote(x_send.at[p, low(c)], x_land.at[p, low(c)], {"head": x_peer}))
+        made[2].start()
+        for_y = partial(y_peer)
+        y_send[p, high(c)] = for_y[half:].astype(jnp.bfloat16)
+        keep_y[c] = for_y[:half]
+        made.append(remote(y_send.at[p, high(c)], y_land.at[p, high(c)], {"head": y_peer}))
+        made[3].start()
+        keep_own[part] = partial(me)
+        scatter_copies[p, c] = made
+
+    def combine(p, c):
+        made = scatter_copies[p, c]
+        made[0].wait_recv()
+        y_send[p, low(c)] = (keep_y[c] + diag_x_land[p, c].astype(jnp.float32)).astype(jnp.bfloat16)
+        made.append(remote(y_send.at[p, low(c)], y_land.at[p, low(c)], {"head": y_peer}))
+        made[4].start()
+        made[1].wait_recv()
+        x_send[p, high(c)] = (keep_x[c] + diag_y_land[p, c].astype(jnp.float32)).astype(jnp.bfloat16)
+        made.append(remote(x_send.at[p, high(c)], x_land.at[p, high(c)], {"head": x_peer}))
+        made[5].start()
+
+    def finish(p, c):
+        made = scatter_copies[p, c]
+        for at in (2, 3, 4, 5):
+            made[at].wait_recv()
+        part = pl.ds(c * chunk, chunk)
+        arrived = x_land[p, part].astype(jnp.float32) + y_land[p, part].astype(jnp.float32)
+        return gathered[p, me, part].astype(jnp.float32) + (keep_own[part] + arrived)
+
+    forward_copies = {}
+
+    def finish_first(c):
+        part = pl.ds(c * chunk, chunk)
+        result = finish(0, c)
+        first_ref[part] = result
+        forward_buf[part] = result.astype(jnp.bfloat16)
+        made = remote(forward_buf.at[part], gathered.at[1, me, part], {"segment": seg + 1})
+        forward_copies[c] = made
+
+        @pl.when(seg < seg_count - 1)
+        def _():
+            made.start()
+
+    def enter(c):
+        @pl.when(seg > 0)
+        def _():
+            forward_copies[c].wait_recv()
+
+        gather_send(1, c)
+
+    def finish_second(c):
+        second_ref[pl.ds(c * chunk, chunk)] = finish(1, c)
+
+    for c in range(row_chunks):
+        gather_send(0, c)
+
+    @pl.when(seg == 0)
+    def _():
+        gathered[1, me] = new_ref[...]
+
+    place = lax.broadcasted_iota(jnp.int32, mask_buf.shape, 1)
+    mask_buf[...] = jnp.where(place < len_ref[0], 0.0, NEGATIVE)
+    new_k[...] = jnp.zeros(new_k.shape, new_k.dtype)
+    new_v[...] = jnp.zeros(new_v.shape, new_v.dtype)
+
+    gather_pass_on(0, 0)
+    project(0, 0)
+    gather_pass_on(0, 1)
+    attend(0, 0)
+    mix(0, 0)
+    project(0, 1)
+    combine(0, 0)
+    attend(0, 1)
+    finish_first(0)
+    mix(0, 1)
+    enter(0)
+    combine(0, 1)
+    gather_pass_on(1, 0)
+    finish_first(1)
+    enter(1)
+    project(1, 0)
+    gather_pass_on(1, 1)
+    attend(1, 0)
+    mix(1, 0)
+    project(1, 1)
+    combine(1, 0)
+    attend(1, 1)
+    finish_second(0)
+    mix(1, 1)
+    combine(1, 1)
+    finish_second(1)
+
+    kept_back = list(forward_copies.values())
+    for made in copies:
+        if not any(made is other for other in kept_back):
+            made.wait_send()
+
+    @pl.when(seg < seg_count - 1)
+    def _():
+        for made in kept_back:
+            made.wait_send()
+
+
+def fused(slices, new_slice, norm_gain, w_query, w_keyval, w_out, cached_rows, lengths):
+    rows, features = slices.shape
+    head_count = lax.axis_size("head")
+    row_chunks = 2
+    chunk = rows // row_chunks
+    half = chunk // 2
+    width = head_count * features
+    query_columns = w_query.shape[2]
+    local_heads = query_columns // HD
+    cached = cached_rows.shape[1]
+    half_dim = HD // 2
+    exponent = jnp.arange(half_dim, dtype=jnp.float32) * (2.0 / HD)
+    inverse = jnp.power(jnp.float32(ROPE_BASE), -exponent)
+    positions = (lengths[0] + jnp.arange(2 * rows, dtype=jnp.int32)).astype(jnp.float32)
+    angles = positions[:, None] * inverse[None, :]
+    cosine = jnp.cos(angles)
+    sine = jnp.sin(angles)
+    cosines = jnp.concatenate([cosine, cosine], axis=1)
+    sines = jnp.concatenate([-sine, sine], axis=1)
+    vmem = pl.BlockSpec(memory_space=pltpu.VMEM)
+    anywhere = pl.BlockSpec(memory_space=pl.ANY)
+    narrow = jnp.bfloat16
+    wide = jnp.float32
+    copy_count = 12 * 2 * row_chunks + row_chunks
+    flops = 4 * rows * width * (w_query.shape[2] * 2 + w_keyval.shape[2]) + 8 * rows * local_heads * HD * cached
+    return pl.pallas_call(
+        functools.partial(exchange_kernel, row_chunks),
+        out_shape=(jax.ShapeDtypeStruct((rows, features), wide),) * 2,
+        in_specs=[vmem] * 5 + [pl.BlockSpec(memory_space=pltpu.SMEM)] + [anywhere] * 4,
+        out_specs=(vmem, vmem),
+        scratch_shapes=[
+            pltpu.VMEM(w_query.shape[1:], narrow),
+            pltpu.VMEM(w_keyval.shape[1:], narrow),
+            pltpu.VMEM(w_out.shape[1:], narrow),
+            pltpu.VMEM(cached_rows.shape[1:], narrow),
+            pltpu.VMEM((2, head_count, rows, features), narrow),
+            pltpu.VMEM((chunk, width), narrow),
+            pltpu.VMEM((local_heads * chunk, HD), narrow),
+            pltpu.VMEM((local_heads * chunk, cached), wide),
+            pltpu.VMEM((1, cached), wide),
+            pltpu.VMEM((2, rows, HD), narrow),
+            pltpu.VMEM((2, rows, HD), narrow),
+            pltpu.VMEM((chunk, query_columns), narrow),
+            pltpu.VMEM((2, rows, features), narrow),
+            pltpu.VMEM((2, rows, features), narrow),
+            pltpu.VMEM((2, rows, features), narrow),
+            pltpu.VMEM((row_chunks, half, features), wide),
+            pltpu.VMEM((row_chunks, half, features), wide),
+            pltpu.VMEM((rows, features), wide),
+            pltpu.VMEM((2, row_chunks, half, features), narrow),
+            pltpu.VMEM((2, row_chunks, half, features), narrow),
+            pltpu.VMEM((2, rows, features), narrow),
+            pltpu.VMEM((2, rows, features), narrow),
+            pltpu.VMEM((rows, features), narrow),
+            pltpu.SemaphoreType.DMA((4,)),
+            pltpu.SemaphoreType.DMA((copy_count,)),
+            pltpu.SemaphoreType.DMA((copy_count,)),
+        ],
+        compiler_params=pltpu.CompilerParams(
+            collective_id=0, has_side_effects=True, vmem_limit_bytes=56 * 1024 * 1024
+        ),
+        cost_estimate=pl.CostEstimate(
+            flops=flops, bytes_accessed=2 * (w_query.size + w_keyval.size + w_out.size + cached_rows.size),
+            transcendentals=2 * rows * local_heads * cached,
+        ),
+    )(slices, new_slice, norm_gain, cosines, sines, lengths, w_query, w_keyval, w_out, cached_rows)
+
+
 def solution(mesh):
     placed = (
         P("segment", "head"),
@@ -203,8 +568,9 @@
         P("segment", "head", None),
         P("segment"),
     )
+    square = mesh.shape["head"] == KVH
     return jax.shard_map(
-        local,
+        fused if square else local,
         mesh=mesh,
         in_specs=placed,
         out_specs=(P("segment", "head"), P("segment", "head")),

time: 281 us -> 63.3 us (0.23)
  waiting for transfers between devices: 168 us -> 0 us
  Pallas kernels: 0 us -> 56.6 us
  matrix products: 49.4 us -> 0 us
  local copies, waits for them, and re-layouts: 26.3 us -> 3.77 us
  other arithmetic: 19.8 us -> 1.39 us
  between operations: 14.8 us -> 1.3 us
    reduce_scatter x2 -> x0, waiting for transfers between devices: 95.8 us -> none  [advance(): lax.psum_scatter(partial_out, 'head', scatter_dimension=1, tiled=True)]
    all_gather x2 -> x0, waiting for transfers between devices: 70.5 us -> none  [advance(): full_rows = lax.all_gather(own_rows, 'head', axis=1, tiled=True)]
    pallas_call x0 -> x1, Pallas kernels: none -> 56.6 us  [fused(): pl.pallas_call(functools.partial(exchange_kernel, row_chunks), out_shape=...]
    dot_general x30 -> x0, matrix products: 49.4 us -> none  [the longest x12 16.9 us: softmax_partial(): jnp.einsum('nrk,kd->nrd', weights.astype(jnp.bfloat16), value_rows, prefe...]
    while x84 -> x0, local copies, waits for them, and re-layouts: 12.2 us -> none
    reduce_sum x14 -> x0, other arithmetic: 7.69 us -> none  [the longest x2 3.94 us: normalize(): mean_square = jnp.mean(rows_in * rows_in, axis=-1, keepdims=True)]
    dot_general x1 -> x0, local copies, waits for them, and re-layouts: 6.43 us -> none  [project(): jnp.dot(normed, query_w, preferred_element_type=jnp.float32)]
    add x14 -> x0, other arithmetic: 4.57 us -> none  [the longest x2 2.99 us: advance(): return (own_rows + summed, recent)]
  transfers between devices with their start and end apart: 5 -> 0, of which waited for: 5 -> 0; matrix products, arithmetic and copies ran while one was open for 4% -> 0% of each run, Pallas kernels for 0% -> 0%
where the time goes in v1:
time: 63.3 us; the launch traced here: 63.1 us
  Pallas kernels  56.6 us (89%)
  local copies, waits for them, and re-layouts  3.77 us (6%)
  other arithmetic  1.39 us (2%)
  between operations  1.3 us (2%)
    pallas_call x1, Pallas kernels, fused(): pl.pallas_call(functools.partial(exchange_kernel, row_chunks), out_shape=...  56.6 us
    unnamed x2, local copies, waits for them, and re-layouts  3.77 us

profile of v1, /device:TPU:0, one launch (start us, length us, event | category | flops | bytes accessed | tf_op | source)
XLA Modules:
  0.0 63.1 jit_solution(1052620568201919588)
XLA Ops:
  1.3 0.5 fusion
  1.8 0.8 %pad_maximum_fusion = (f32[256,128]{1,0:T(8,128)}, f32[256,128]{1,0:T(8,128)}) fusion(f32[256,64]{1,0:T(8,128)S(1)} %get-tuple-element.4, f32[256,64]{1,0:T(8,128)S(1)} %get-tuple-element.3, f32[256,64]{1,0:T(8,128)S(1)} %get-tuple-element.2), kind=kLoop, calls=%fused_computation.2 | loop fusion | flops 65536 | bytes 458752 | tf_op jit(solution)/shard_map/concatenate | solution.py:509
  2.7 56.6 %shard_map.95 = (f32[128,1024]{1,0:T(8,128)}, f32[128,1024]{1,0:T(8,128)}) custom-call(bf16[128,1024]{1,0:T(8,128)(2,1)} %x_ref.1, bf16[128,1024]{1,0:T(8,128)(2,1)} %new_ref.1, f32[1,4096]{1,0:T(1,128)} %gain_ref.1, f32[256,128]{1,0:T(8,128)} %get-tuple-element.5.cos_ref, f32[256,128]{1,0:T(8,128)} %get-tuple-element.6.sin_ref, s32[1]{0:T(128)} %copy.12.len_ref, ...), custom_call_target="tpu_custom_call" | custom-call | flops 4831838208 | bytes 12582912 | tf_op jit(solution)/shard_map/pallas_call | solution.py:517
  59.3 1.9 %copy.13 = f32[128,1024]{1,0:T(8,128)} copy(f32[128,1024]{1,0:T(8,128)} %get-tuple-element.9) | data formatting | bytes 1048576
  61.2 1.9 %copy.14 = f32[128,1024]{1,0:T(8,128)} copy(f32[128,1024]{1,0:T(8,128)} %get-tuple-element.10) | data formatting | bytes 1048576
  (2 shorter events, 0.0 us)
